TPU v7x, 32 devices: a whole 2x2x4 slice. The times are simulated.
32 devices in a mesh: groups: 1, node: 8 (over z, y), local: 4 (over x, core).
Axes of the slice: x: 2, y: 2, z: 4, core: 2. Of those that a mesh axis runs over, the one named last changes fastest.
Arguments:
- tokens: bfloat16 [4096, 2048], P(('groups', 'node', 'local')), may hold values from -6 to 6
- out_grad: bfloat16 [4096, 2048], P(('groups', 'node', 'local')), may hold values from -6 to 6
- routes: int32 [4096, 6], P(('groups', 'node', 'local')), may hold values from 0 to 15, all different within a row; in each aligned block of 128 rows (0 to 127, 128 to 255, ...) at most 72 rows name the same one
- route_weight: float32 [4096, 6], P(('groups', 'node', 'local')), may hold values from 0.02 to 0.4
- example_id: int32 [4096], P(('groups', 'node', 'local')), may hold values from 0 to 7, never falling along the last dimension, each value on 1 to 1024 neighbouring positions
- gate_weight: bfloat16 [32, 2048, 704], P(('node', 'local')), may hold values from -0.125 to 0.125
- up_weight: bfloat16 [32, 2048, 704], P(('node', 'local')), may hold values from -0.125 to 0.125
- hidden_basis: bfloat16 [32, 704, 64], P(('node', 'local')), may hold values from -0.15625 to 0.15625
- model_basis: bfloat16 [32, 1024, 64], P(('node', 'local')), may hold values from -0.125 to 0.125
Outputs:
- logged: float32 [16, 8, 64, 64], P('node', ('groups', 'local'))
Inputs may be any that keep to these rules, and one draw needn't show every extreme that they name: `routes`: each token names 6 different experts. Within the 128 tokens of one device (aligned blocks), no expert is named more than 72 times, a bound that some block reaches. `example_id`: never falls along the tokens; each example holds 1 to 1024 tokens.
All inputs are finite; a program needn't handle non-finite values.
Results may differ from a plain program's by a relative error of at most 0.0041.
Values may be sent and summed in bfloat16 or wider, within the bound.
A program may use at most 128 MiB of HBM per device.

v0:
```python
import jax
import jax.numpy as jnp
from jax import lax
from jax.sharding import PartitionSpec as P


def swapped(block, axis, stride):
    count = lax.axis_size(axis)
    route = []
    for low in range(count):
        high = low | 1 << stride
        if high != low and high < count:
            route += [(low, high), (high, low)]
    return lax.ppermute(block, axis, route)


def local(
    tokens,
    out_grad,
    routes,
    route_weight,
    example_id,
    gate_weight,
    up_weight,
    hidden_basis,
    model_basis,
):
    node_count = lax.axis_size("node")
    local_count = lax.axis_size("local")
    experts = node_count * local_count // 2
    per_node = local_count // 2
    tok_rows, model_width = tokens.shape
    top_count = routes.shape[1]
    capacity = 3 * tok_rows * top_count // (2 * experts)
    half_width = model_width // 2
    examples = 2 * local_count
    rank_size = hidden_basis.shape[2]
    flat_routes = routes.reshape(-1)
    expert_ids = jnp.arange(experts, dtype=jnp.int32)
    chosen = (flat_routes[:, None] == expert_ids[None, :]).astype(jnp.int32)
    earlier = jnp.cumsum(chosen, axis=0) - chosen
    placing = jnp.sum(earlier * chosen, axis=1)
    target = flat_routes * capacity + placing
    owner_row = (
        jnp.full((experts * capacity,), -1, jnp.int32)
        .at[target]
        .set(jnp.arange(tok_rows * top_count, dtype=jnp.int32))
    )
    filled = owner_row >= 0
    source = jnp.maximum(owner_row, 0)
    token_of = source // top_count
    weight_of = jnp.where(filled, route_weight.reshape(-1)[source], jnp.zeros((), jnp.float32))
    sent_rows = jnp.where(filled[:, None], tokens[token_of], jnp.zeros((), tokens.dtype))
    sent_grads = (weight_of[:, None] * out_grad[token_of].astype(jnp.float32)).astype(jnp.bfloat16)
    sent_examples = example_id[token_of].astype(jnp.bfloat16)
    grid_feats = jnp.repeat(sent_rows.reshape(experts, capacity, model_width), 2, axis=0)
    grid_grads = (
        sent_grads.reshape(experts, capacity, 2, half_width)
        .transpose(0, 2, 1, 3)
        .reshape(2 * experts, capacity, half_width)
    )
    grid_examples = jnp.repeat(sent_examples.reshape(experts, capacity), 2, axis=0)
    row_feats = lax.all_to_all(
        grid_feats, ("node", "local"), split_axis=0, concat_axis=0, tiled=True
    )
    row_grads = lax.all_to_all(
        grid_grads, ("node", "local"), split_axis=0, concat_axis=0, tiled=True
    )
    row_examples = lax.all_to_all(
        grid_examples, ("node", "local"), split_axis=0, concat_axis=0, tiled=True
    )
    leading = row_feats.shape[:2]
    flat_feats = row_feats.reshape(-1, model_width)
    gate_proj = jnp.dot(flat_feats, gate_weight[0], preferred_element_type=jnp.float32)
    up_proj = jnp.dot(flat_feats, up_weight[0], preferred_element_type=jnp.float32)
    hidden = (jax.nn.silu(gate_proj) * up_proj).astype(jnp.bfloat16)
    left_side = jnp.dot(hidden, hidden_basis[0], preferred_element_type=jnp.float32)
    right_part = jnp.dot(
        row_grads.reshape(-1, half_width), model_basis[0], preferred_element_type=jnp.float32
    )
    left_side, right_part, arrived = (
        left_side.reshape(leading + (rank_size,)),
        right_part.reshape(leading + (rank_size,)),
        row_examples,
    )
    right_side = right_part + swapped(right_part, "local", 0)
    flat_left = left_side.reshape(-1, rank_size)
    flat_right = right_side.reshape(-1, rank_size)
    flat_examples = arrived.reshape(-1).astype(jnp.int32)
    member = (flat_examples[:, None] == jnp.arange(examples, dtype=jnp.int32)[None, :]).astype(
        jnp.float32
    )
    spread = (member[:, :, None] * flat_left[:, None, :]).reshape(
        flat_left.shape[0], examples * rank_size
    )
    logged_own = lax.dot_general(
        spread,
        flat_right,
        (((0,), (0,)), ((), ())),
        precision=lax.Precision.HIGHEST,
        preferred_element_type=jnp.float32,
    ).reshape(examples, rank_size, rank_size)
    slot_in_node = lax.axis_index("local") // 2
    chooser = (jnp.arange(per_node, dtype=jnp.int32) == slot_in_node).astype(jnp.float32)
    padded_term = chooser[:, None, None, None] * logged_own[None]
    return lax.psum_scatter(padded_term, "local", scatter_dimension=1, tiled=True)


def solution(mesh):
    in_specs = (
        P(("groups", "node", "local"), None),
        P(("groups", "node", "local"), None),
        P(("groups", "node", "local"), None),
        P(("groups", "node", "local"), None),
        P(("groups", "node", "local")),
        P(("node", "local"), None, None),
        P(("node", "local"), None, None),
        P(("node", "local"), None, None),
        P(("node", "local"), None, None),
    )
    out_specs = P("node", ("groups", "local"), None, None)
    return jax.shard_map(local, mesh=mesh, in_specs=in_specs, out_specs=out_specs, check_vma=False)
```

profile of v0, /device:TPU:0, one launch (start us, length us, event | category | flops | bytes accessed | tf_op | source)
XLA Modules:
  0.0 464.8 jit_solution(9571611802203011762)
XLA Ops:
  6.5 0.9 copy.26
  7.8 0.7 broadcast_multiply_fusion.1
  8.5 1.7 reduce-window.6
  10.2 0.3 slice_reduce_fusion
  10.9 3.4 scatter_custom_fusion
  14.3 7.0 %gather_fusion = s32[1152]{0:T(1024)S(1)} fusion(s32[128]{0:T(128)S(1)} %copy-done.1, s32[2048]{0:T(1024)S(1)} %get-tuple-element.10), kind=kCustom, calls=%fused_computation | custom fusion | bytes 13824 | tf_op jit(solution)/shard_map/gather | solution.py:55
  21.4 0.6 copy.29
  22.0 7.3 %all-to-all-start = ((bf16[32,1,72]{2,1,0:T(2,128)(2,1)}), bf16[32,1,72]{2,1,0:T(2,128)(2,1)S(1)}, u32[]{:S(2)}, u32[]{:S(2)}) async-start(bf16[32,1,72]{2,1,0:T(2,128)(2,1)} %copy.29), calls=%async_computation | async-start | bytes 32768 | tf_op jit(solution)/shard_map/all_to_all | solution.py:69
  29.6 4.6 gather_fusion.2
  34.3 5.9 %gather_fusion.3 = bf16[1152,2048]{1,0:T(8,128)(2,1)} fusion(bf16[128,2048]{1,0:T(8,128)(2,1)S(1)} %copy-done.2, s32[2048]{0:T(1024)S(1)} %get-tuple-element.10), kind=kCustom, calls=%fused_computation.3 | custom fusion | bytes 9441792 | tf_op jit(solution)/shard_map/gather | solution.py:54
  40.2 12.9 %reshape.145 = f32[16,72,2,1024]{3,2,1,0:T(2,128)} reshape(bf16[1152,2048]{1,0:T(8,128)(2,1)} %gather_fusion.3) | data formatting | bytes 14155776 | tf_op jit(solution)/shard_map/convert_element_type | solution.py:54
  53.1 9.2 %fusion = bf16[16,72,2,1024]{3,1,2,0:T(8,128)(2,1)} fusion(f32[16,72,2,1024]{3,2,1,0:T(2,128)} %reshape.145, f32[16,72]{1,0:T(8,128)S(1)} %mul.78), kind=kLoop, calls=%fused_computation.6 | loop fusion | flops 4718592 | bytes 14160384 | tf_op jit(solution)/shard_map/convert_element_type | solution.py:54
  62.3 5.9 %all-to-all-start.2 = ((bf16[32,72,1024]{2,1,0:T(8,128)(2,1)}), bf16[32,72,1024]{2,1,0:T(8,128)(2,1)}, u32[]{:S(2)}, u32[]{:S(2)}) async-start(bf16[32,72,1024]{2,1,0:T(8,128)(2,1)} %bitcast.60), calls=%async_computation.2 | async-start | bytes 9437184 | tf_op jit(solution)/shard_map/all_to_all | solution.py:66
  68.3 6.0 %gather_fusion.1 = bf16[1152,2048]{1,0:T(8,128)(2,1)} fusion(bf16[128,2048]{1,0:T(8,128)(2,1)S(1)} %copy-done.3, s32[2048]{0:T(1024)S(1)} %get-tuple-element.10), kind=kCustom, calls=%fused_computation.1 | custom fusion | bytes 9441792 | tf_op jit(solution)/shard_map/gather | solution.py:53
  74.4 4.9 %broadcast_select_fusion = bf16[16,72,2048]{2,1,0:T(8,128)(2,1)} fusion(bf16[16,72,2048]{2,1,0:T(8,128)(2,1)} %bitcast.61, pred[16,72]{1,0:T(8,128)(4,1)S(1)} %broadcast_in_dim.46), kind=kLoop, calls=%fused_computation.11 | loop fusion | flops 2359296 | bytes 9438336 | tf_op jit(solution)/shard_map/jit(_where)/select_n | solution.py:53
  79.2 94.3 %all-to-all-done.2 = bf16[32,72,1024]{2,1,0:T(8,128)(2,1)} async-done(((bf16[32,72,1024]{2,1,0:T(8,128)(2,1)}), bf16[32,72,1024]{2,1,0:T(8,128)(2,1)}, u32[]{:S(2)}, u32[]{:S(2)}) %all-to-all-start.2) | async-done | bytes 4718624 | tf_op jit(solution)/shard_map/all_to_all | solution.py:66
  173.5 7.5 %broadcast_in_dim.49 = bf16[16,2,72,2048]{3,2,1,0:T(8,128)(2,1)} broadcast(bf16[16,72,2048]{2,1,0:T(8,128)(2,1)} %broadcast_select_fusion), dimensions={0,2,3} | broadcast | bytes 14155776 | tf_op jit(solution)/shard_map/broadcast_in_dim | solution.py:56
  181.1 3.9 all-to-all-start.1
  185.0 0.2 all-reduce.3.cloned.1.call-start
  185.4 4.5 fusion.12
  189.9 0.2 collective-permute-start
  190.2 2.5 collective-permute-done
  192.8 1.6 copy.32
  194.4 1.8 reshape.191
  196.1 198.0 %all-to-all-done.1 = bf16[32,72,2048]{2,1,0:T(8,128)(2,1)} async-done(((bf16[32,72,2048]{2,1,0:T(8,128)(2,1)}), bf16[32,72,2048]{2,1,0:T(8,128)(2,1)}, u32[]{:S(2)}, u32[]{:S(2)}) %all-to-all-start.1) | async-done | bytes 9437216 | tf_op jit(solution)/shard_map/all_to_all | solution.py:63
  394.1 11.9 %fusion.8 = f32[2304,704]{0,1:T(8,128)} fusion(bf16[2304,2048]{1,0:T(8,128)(2,1)} %bitcast.4, bf16[1,2048,704]{1,2,0:T(8,128)(2,1)S(1)} %copy-done), kind=kOutput, calls=%fused_computation.15 | convolution fusion | flops 6643777536 | bytes 18808832 | tf_op jit(solution)/shard_map/dot_general | solution.py:74
  406.0 14.9 %fusion.4 = f32[2304,64]{0,1:T(8,128)} fusion(f32[2304,704]{0,1:T(8,128)} %fusion.8, bf16[2304,2048]{1,0:T(8,128)(2,1)} %bitcast.4, bf16[1,2048,704]{1,2,0:T(8,128)(2,1)} %param.15, bf16[1,704,64]{1,2,0:T(8,128)(2,1)} %param.16), kind=kOutput, calls=%fused_computation.12 | convolution fusion | flops 6861127680 | bytes 19488768 | tf_op jit(solution)/shard_map/dot_general | solution.py:77
  420.9 4.9 %fusion.1 = f32[8,64,64]{2,1,0:T(8,128)S(1)} fusion(f32[2304,64,1]{0,1,2:T(8,128)S(1)} %reshape.191, f32[2304,64]{0,1:T(8,128)} %fusion.4, f32[2304,8]{0,1:T(8,128)S(1)} %fusion.15), kind=kOutput, calls=%fused_computation.8 | convolution fusion | flops 907149312 | bytes 1384448 | tf_op jit(solution)/shard_map/dot_general | solution.py:96
  425.8 0.9 broadcast_multiply_fusion
  426.8 0.6 dynamic-slice
  428.0 28.4 %all-reduce.3.cloned.1.call-done = f32[2,8,64,64]{3,2,1,0:T(8,128)} async-done(((f32[2,8,64,64]{3,2,1,0:T(8,128)}), f32[2,8,64,64]{3,2,1,0:T(8,128)}) %all-reduce.3.cloned.1.call-update) | async-done | bytes 262160
  456.4 1.6 constant_dynamic-slice_fusion
  (40 shorter events, 1.6 us)
Async XLA Ops:
  6.5 387.6 %copy-start = (bf16[1,2048,704]{1,2,0:T(8,128)(2,1)S(1)}, bf16[1,2048,704]{1,2,0:T(8,128)(2,1)}, u32[]{:S(2)}) copy-start(bf16[1,2048,704]{1,2,0:T(8,128)(2,1)} %param.14) | copy-start | bytes 8650756
  6.5 7.7 %copy-start.1 = (s32[128]{0:T(128)S(1)}, s32[128]{0:T(128)}, u32[]{:S(2)}) copy-start(s32[128]{0:T(128)} %param.13) | copy-start | bytes 1540
  6.5 22.8 %copy-start.5 = (f32[128,6]{0,1:T(8,128)S(1)}, f32[128,6]{0,1:T(8,128)}, u32[]{:S(2)}) copy-start(f32[128,6]{0,1:T(8,128)} %param.12) | copy-start | bytes 9220
  21.3 13.0 %copy-start.2 = (bf16[128,2048]{1,0:T(8,128)(2,1)S(1)}, bf16[128,2048]{1,0:T(8,128)(2,1)}, u32[]{:S(2)}) copy-start(bf16[128,2048]{1,0:T(8,128)(2,1)} %param.10) | copy-start | bytes 1572868
  22.0 40.3 %all-to-all-start = ((bf16[32,1,72]{2,1,0:T(2,128)(2,1)}), bf16[32,1,72]{2,1,0:T(2,128)(2,1)S(1)}, u32[]{:S(2)}, u32[]{:S(2)}) async-start(bf16[32,1,72]{2,1,0:T(2,128)(2,1)} %copy.29), calls=%async_computation | async-start | bytes 32768 | tf_op jit(solution)/shard_map/all_to_all | solution.py:69
  62.3 6.1 %copy-start.3 = (bf16[128,2048]{1,0:T(8,128)(2,1)S(1)}, bf16[128,2048]{1,0:T(8,128)(2,1)}, u32[]{:S(2)}) copy-start(bf16[128,2048]{1,0:T(8,128)(2,1)} %param.9) | copy-start | bytes 1572868
  62.3 111.3 %all-to-all-start.2 = ((bf16[32,72,1024]{2,1,0:T(8,128)(2,1)}), bf16[32,72,1024]{2,1,0:T(8,128)(2,1)}, u32[]{:S(2)}, u32[]{:S(2)}) async-start(bf16[32,72,1024]{2,1,0:T(8,128)(2,1)} %bitcast.60), calls=%async_computation.2 | async-start | bytes 9437184 | tf_op jit(solution)/shard_map/all_to_all | solution.py:66
  181.1 4.3 copy-start.4
  181.1 213.0 %all-to-all-start.1 = ((bf16[32,72,2048]{2,1,0:T(8,128)(2,1)}), bf16[32,72,2048]{2,1,0:T(8,128)(2,1)}, u32[]{:S(2)}, u32[]{:S(2)}) async-start(bf16[32,72,2048]{2,1,0:T(8,128)(2,1)} %bitcast.59), calls=%async_computation.1 | async-start | bytes 18874368 | tf_op jit(solution)/shard_map/all_to_all | solution.py:63
  185.0 271.4 %all-reduce.3.cloned.1.call-start = ((), (), s32[]{:S(2)}) async-start(), calls=%async_computation.3 | async-start | bytes 1048576
  189.9 2.7 collective-permute-start
  406.0 20.7 %copy-start.6 = (u32[32]{0:T(128)S(1)}, u32[32]{0:T(128)}, u32[]{:S(2)}) copy-start(u32[32]{0:T(128)} %constant.55) | copy-start | bytes 388
Sparse Core Ops, SparseCore 0:
  426.9 29.4 all-reduce.2
where the time goes:
time: 466 us; the launch traced here: 465 us
  waiting for transfers between devices  323 us (69%)
  local copies, waits for them, and re-layouts  55.8 us (12%)
  matrix products  36.2 us (8%)
  other arithmetic  17.7 us (4%)
  starting transfers between devices  17.6 us (4%)
  between operations  14.3 us (3%)
    all_to_all x1, waiting for transfers between devices, local(): lax.all_to_all(grid_feats, ('node', 'local'), split_axis=0, concat_axis=0...  198 us
    all_to_all x1, waiting for transfers between devices, local(): lax.all_to_all(grid_grads, ('node', 'local'), split_axis=0, concat_axis=0...  94.3 us
    unnamed x2, waiting for transfers between devices  28.4 us
    dot_general x1, matrix products, local(): jnp.dot(hidden, hidden_basis[0], preferred_element_type=jnp.float32)  14.9 us
    convert_element_type x1, local copies, waits for them, and re-layouts, local(): out_grad[token_of].astype(jnp.float32)  12.9 us
    dot_general x1, matrix products, local(): jnp.dot(flat_feats, gate_weight[0], preferred_element_type=jnp.float32)  11.9 us
  transfers between devices with their start and end apart: 5, of which 4 were waited for; matrix products, arithmetic and copies ran while one was open for 11% of the time, Pallas kernels for 0%

commit v1 on v0

--- a/solution.py
+++ b/solution.py
@@ -1,7 +1,13 @@
+import functools
+
 import jax
 import jax.numpy as jnp
 from jax import lax
+from jax.experimental import pallas as pl
+from jax.experimental.pallas import tpu as pltpu
 from jax.sharding import PartitionSpec as P
+
+MESH = pl.DeviceIdType.MESH
 
 
 def swapped(block, axis, stride):
@@ -106,7 +112,385 @@
     return lax.psum_scatter(padded_term, "local", scatter_dimension=1, tiled=True)
 
 
+def fused_kernel(
+    tok_ref,
+    grad_ref,
+    coef_ref,
+    aux_ref,
+    gate_ref,
+    up_ref,
+    hid_ref,
+    basis_ref,
+    out_ref,
+    tbuf,
+    qbuf,
+    rmsg,
+    rbuf,
+    lbuf,
+    acc,
+    fsend,
+    fbuf,
+    own_sem,
+    t_send,
+    t_recv,
+    ts_recv,
+    q_send,
+    q_recv,
+    qs_recv,
+    r_send,
+    r_recv,
+    rs_sem,
+    f_send,
+    f_recv,
+):
+    group = lax.axis_index("groups")
+    node = lax.axis_index("node")
+    spot = lax.axis_index("local")
+    depth = lax.axis_size("node") // 2
+    chips = 2 * lax.axis_size("node")
+    pairs = lax.axis_size("local")
+    zi, yi = node // 2, node % 2
+    xi, core = spot // 2, spot % 2
+    me = node * 2 + xi
+    half = grad_ref.shape[1] // 2
+    rank = hid_ref.shape[0]
+    rows = tok_ref.shape[0]
+
+    def device(z, y, x, c):
+        return (group, z * 2 + y, x * 2 + c)
+
+    first_x, first_y = 1 - core, core
+    up = device(lax.rem(zi + 1, depth), yi, xi, core)
+    down = device(lax.rem(zi + depth - 1, depth), yi, xi, core)
+    near = device(zi, (yi + first_y) % 2, (xi + first_x) % 2, core)
+    far = device(zi, (yi + first_x) % 2, (xi + first_y) % 2, core)
+    twin = device(zi, yi, xi, 1 - core)
+
+    barrier = pltpu.get_barrier_semaphore()
+
+    @pl.loop(1, chips)
+    def _(step):
+        chip = (me + step) % chips
+        pl.semaphore_signal(
+            barrier, inc=1, device_id=(group, chip // 2, (chip % 2) * 2 + core), device_id_type=MESH
+        )
+
+    for c in (0, 1):
+        where = device(zi, yi, (xi + c) % 2, 1 - core)
+        pl.semaphore_signal(barrier, inc=1, device_id=where, device_id_type=MESH)
+    pl.semaphore_wait(barrier, chips + 1)
+
+    def place(idx):
+        k, pos = idx // 4, idx % 4
+        one, two = pos % 2, pos // 2
+        away = (k + 1) // 2
+        dz = away * (1 - 2 * (k % 2))
+        oz = zi + dz
+        valid = (oz >= 0) & (oz < depth)
+        oz = jnp.clip(oz, 0, depth - 1)
+        flip_x = one * first_x + two * first_y
+        flip_y = one * first_y + two * first_x
+        origin = (oz * 2 + (yi + flip_y) % 2) * 2 + (xi + flip_x) % 2
+        return origin, valid, one, two, dz
+
+    def links(idx, view, send, recv, twin_recv):
+        origin, valid, one, two, dz = place(idx)
+        straight = valid & (one == 0) & (two == 0)
+        plan = (
+            (straight & (dz <= 0) & (zi < depth - 1), up, recv),
+            (straight & (dz >= 0) & (zi > 0), down, recv),
+            (valid & (two == 0), far, recv),
+            (straight, near, recv),
+            (valid, twin, twin_recv),
+        )
+        for j, (wanted, where, sem) in enumerate(plan):
+            copy = pltpu.make_async_remote_copy(
+                src_ref=view(origin, core),
+                dst_ref=view(origin, core),
+                send_sem=send.at[origin, j],
+                recv_sem=sem.at[origin],
+                device_id=where,
+                device_id_type=MESH,
+            )
+            yield wanted, copy
+
+    def arrival(view, origin, c, send, sem):
+        return pltpu.make_async_remote_copy(
+            src_ref=view(origin, c),
+            dst_ref=view(origin, c),
+            send_sem=send.at[0, 0],
+            recv_sem=sem.at[origin],
+            device_id=twin,
+            device_id_type=MESH,
+        )
+
+    def forward(idx, view, send, recv, twin_recv):
+        origin, valid, *_ = place(idx)
+
+        @pl.when(valid & (idx > 0))
+        def _():
+            arrival(view, origin, core, send, recv).wait_recv()
+
+        for wanted, copy in links(idx, view, send, recv, twin_recv):
+            pl.when(wanted)(copy.start)
+
+    def finish(idx, view, send, recv, twin_recv):
+        for wanted, copy in links(idx, view, send, recv, twin_recv):
+            pl.when(wanted)(copy.wait_send)
+
+    def t_view(origin, c):
+        return tbuf.at[origin, c]
+
+    def q_view(origin, c):
+        return qbuf.at[c, origin]
+
+    t_all = (t_view, t_send, t_recv, ts_recv)
+    q_all = (q_view, q_send, q_recv, qs_recv)
+    positions = 4 * (2 * depth - 1)
+
+    own_q = pltpu.make_async_copy(basis_ref, qbuf.at[core, me], own_sem.at[0])
+    own_t = pltpu.make_async_copy(tok_ref, tbuf.at[me, core], own_sem.at[1])
+    own_q.start()
+    own_t.start()
+    own_q.wait()
+
+    @pl.loop(0, positions)
+    def _(idx):
+        forward(idx, *q_all)
+
+    own_t.wait()
+    forward(0, *t_all)
+
+    @pl.loop(0, chips)
+    def _(chip):
+        arrival(q_view, chip, 1 - core, q_send, qs_recv).wait_recv()
+
+    @pl.loop(0, chips)
+    def _(chip):
+        total = None
+        for h in (0, 1):
+            block = qbuf[h, chip]
+            twice = jnp.concatenate([block, block], axis=0)
+            term = lax.dot_general(
+                grad_ref[:, h * half : (h + 1) * half],
+                twice,
+                (((1,), (1,)), ((), ())),
+                preferred_element_type=jnp.float32,
+            )
+            total = term if total is None else total + term
+        lanes = lax.broadcasted_iota(jnp.int32, coef_ref.shape, 1)
+        column = jnp.sum(jnp.where(lanes == chip, coef_ref[...], 0.0), axis=1, keepdims=True)
+        rmsg[chip, :rows] = (total * column).astype(jnp.bfloat16)
+        rmsg[chip, rows:] = aux_ref[...]
+
+    def r_copy(chip):
+        return pltpu.make_async_remote_copy(
+            src_ref=rmsg.at[chip],
+            dst_ref=rbuf.at[core, me],
+            send_sem=r_send.at[chip],
+            recv_sem=r_recv.at[me],
+            device_id=(group, chip // 2, (chip % 2) * 2 + core),
+            device_id_type=MESH,
+        )
+
+    own_r = pltpu.make_async_copy(rmsg.at[me], rbuf.at[core, me], own_sem.at[2])
+    own_r.start()
+
+    @pl.loop(1, chips)
+    def _(step):
+        r_copy((me + step) % chips).start()
+
+    def compute(origin):
+        feats = tbuf[origin].reshape(2 * rows, tok_ref.shape[1])
+        gate = jnp.dot(feats, gate_ref[...], preferred_element_type=jnp.float32)
+        upper = jnp.dot(feats, up_ref[...], preferred_element_type=jnp.float32)
+        hidden = (gate / (1.0 + jnp.exp(-gate)) * upper).astype(jnp.bfloat16)
+        left = lax.dot_general(
+            hid_ref[...],
+            hidden,
+            (((1,), (1,)), ((), ())),
+            preferred_element_type=jnp.float32,
+        )
+        high = left.astype(jnp.bfloat16)
+        low = (left - high.astype(jnp.float32)).astype(jnp.bfloat16)
+        lbuf[origin, :rank] = high
+        lbuf[origin, rank:] = low
+
+    lag = 2
+
+    @pl.loop(0, positions + lag)
+    def _(idx):
+        @pl.when((idx > 0) & (idx < positions))
+        def _():
+            forward(idx, *t_all)
+
+        earlier = jnp.maximum(idx - lag, 0)
+        origin, valid, *_ = place(earlier)
+
+        @pl.when(valid & (idx >= lag))
+        def _():
+            arrival(t_view, origin, 1 - core, t_send, ts_recv).wait_recv()
+            compute(origin)
+
+    own_r.wait()
+
+    @pl.loop(1, chips)
+    def _(step):
+        chip = (me + step) % chips
+        pltpu.make_async_remote_copy(
+            src_ref=rmsg.at[chip],
+            dst_ref=rbuf.at[core, chip],
+            send_sem=r_send.at[chip],
+            recv_sem=r_recv.at[chip],
+            device_id=twin,
+            device_id_type=MESH,
+        ).wait_recv()
+
+    share = pltpu.make_async_remote_copy(
+        src_ref=rbuf.at[core],
+        dst_ref=rbuf.at[core],
+        send_sem=rs_sem.at[0],
+        recv_sem=rs_sem.at[1],
+        device_id=twin,
+        device_id_type=MESH,
+    )
+    share.start()
+    share.wait_recv()
+
+    acc[...] = jnp.zeros_like(acc)
+
+    @pl.loop(0, chips)
+    def _(chip):
+        token = lax.broadcasted_iota(jnp.int32, (rows, 2 * rank), 0).astype(jnp.float32)
+        parts = []
+        for c in (0, 1):
+            right = rbuf[c, chip, :rows].astype(jnp.float32)
+            bounds = rbuf[c, chip, rows:].astype(jnp.float32)
+            cols = []
+            for p in range(pairs):
+                inside = (token >= bounds[p : p + 1]) & (token < bounds[pairs + p : pairs + p + 1])
+                cols.append(jnp.where(inside, right, 0.0).astype(jnp.bfloat16))
+            parts.append(jnp.concatenate(cols, axis=1))
+        spread = jnp.concatenate(parts, axis=0)
+        acc[...] += jnp.dot(lbuf[chip], spread, preferred_element_type=jnp.float32)
+
+    width = 2 * rank
+    for p in range(pairs):
+        cut = slice(p * width, (p + 1) * width)
+        fsend[p] = acc[:rank, cut] + acc[rank:, cut]
+    fbuf[spot] = fsend[spot]
+
+    def f_copy(step, source):
+        peer = (spot + step) % pairs
+        return pltpu.make_async_remote_copy(
+            src_ref=fsend.at[peer],
+            dst_ref=fbuf.at[peer if source else spot],
+            send_sem=f_send.at[peer],
+            recv_sem=f_recv.at[peer if source else spot],
+            device_id=(group, node, peer),
+            device_id_type=MESH,
+        )
+
+    for step in range(1, pairs):
+        f_copy(step, False).start()
+    for step in range(1, pairs):
+        f_copy(step, True).wait_recv()
+    for e in range(pairs // 2):
+        out_ref[e] = fbuf[2 * e] + fbuf[2 * e + 1]
+
+    for step in range(1, pairs):
+        f_copy(step, False).wait_send()
+    share.wait_send()
+
+    @pl.loop(1, chips)
+    def _(step):
+        r_copy((me + step) % chips).wait_send()
+
+    @pl.loop(0, positions)
+    def _(idx):
+        finish(idx, *q_all)
+        finish(idx, *t_all)
+
+
+def fused_local(
+    tokens,
+    out_grad,
+    routes,
+    route_weight,
+    example_id,
+    gate_weight,
+    up_weight,
+    hidden_basis,
+    model_basis,
+):
+    local_count = lax.axis_size("local")
+    chips = lax.axis_size("node") * local_count // 2
+    examples = 2 * local_count
+    rows, width = tokens.shape
+    half_width = hidden_basis.shape[1]
+    rank = hidden_basis.shape[2]
+    chosen = routes[:, :, None] == jnp.arange(chips, dtype=jnp.int32)
+    coef = jnp.sum(jnp.where(chosen, route_weight[:, :, None], 0.0), axis=1)
+    before = jnp.sum(
+        example_id[None, :] < jnp.arange(examples + 1, dtype=jnp.int32)[:, None], axis=1
+    )
+    low = jnp.repeat(before[:-1], rank).reshape(local_count, 2 * rank)
+    high = jnp.repeat(before[1:], rank).reshape(local_count, 2 * rank)
+    fill = jnp.zeros((16 - 2 * local_count, 2 * rank), low.dtype)
+    aux = jnp.concatenate([low, high, fill]).astype(jnp.bfloat16)
+    vmem = pl.BlockSpec(memory_space=pltpu.VMEM)
+    dma = pltpu.SemaphoreType.DMA
+    bf16, f32 = jnp.bfloat16, jnp.float32
+    flops = 2 * 2 * rows * chips * width * 2 * half_width
+    logged = pl.pallas_call(
+        fused_kernel,
+        out_shape=jax.ShapeDtypeStruct((local_count // 2, rank, 2 * rank), f32),
+        in_specs=[vmem] * 8,
+        out_specs=vmem,
+        scratch_shapes=[
+            pltpu.VMEM((chips, 2, rows, width), bf16),
+            pltpu.VMEM((2, chips, rank, width // 2), bf16),
+            pltpu.VMEM((chips, rows + 16, 2 * rank), bf16),
+            pltpu.VMEM((2, chips, rows + 16, 2 * rank), bf16),
+            pltpu.VMEM((chips, 2 * rank, 2 * rows), bf16),
+            pltpu.VMEM((2 * rank, examples * rank), f32),
+            pltpu.VMEM((local_count, rank, 2 * rank), f32),
+            pltpu.VMEM((local_count, rank, 2 * rank), f32),
+            dma((3,)),
+            dma((chips, 5)),
+            dma((chips,)),
+            dma((chips,)),
+            dma((chips, 5)),
+            dma((chips,)),
+            dma((chips,)),
+            dma((chips,)),
+            dma((chips,)),
+            dma((2,)),
+            dma((local_count,)),
+            dma((local_count,)),
+        ],
+        compiler_params=pltpu.CompilerParams(
+            collective_id=0, has_side_effects=True, vmem_limit_bytes=56 * 1024 * 1024
+        ),
+        cost_estimate=pl.CostEstimate(flops=flops, bytes_accessed=1 << 23, transcendentals=0),
+    )(
+        tokens,
+        out_grad,
+        coef,
+        aux,
+        gate_weight[0],
+        up_weight[0],
+        hidden_basis[0].T,
+        model_basis[0].T,
+    )
+    logged = logged.reshape(local_count // 2, rank, 2, rank)
+    return logged.transpose(0, 2, 1, 3)
+
+
 def solution(mesh):
+    sizes = dict(mesh.shape)
+    small = sizes["node"] == 8 and sizes["local"] == 4
+    body = fused_local if small else local
     in_specs = (
         P(("groups", "node", "local"), None),
         P(("groups", "node", "local"), None),
@@ -119,4 +503,4 @@
         P(("node", "local"), None, None),
     )
     out_specs = P("node", ("groups", "local"), None, None)
-    return jax.shard_map(local, mesh=mesh, in_specs=in_specs, out_specs=out_specs, check_vma=False)
+    return jax.shard_map(body, mesh=mesh, in_specs=in_specs, out_specs=out_specs, check_vma=False)

time: 466 us -> 186 us (0.40)
  waiting for transfers between devices: 323 us -> 0 us
  Pallas kernels: 0 us -> 173 us
  local copies, waits for them, and re-layouts: 55.8 us -> 10.4 us
  matrix products: 36.2 us -> 0 us
  starting transfers between devices: 17.6 us -> 0 us
  other arithmetic: 17.7 us -> 2.39 us
  between operations: 14.3 us -> 0.03 us
    all_to_all x3 -> x0, waiting for transfers between devices: 292 us -> none  [the longest x1 198 us: local(): lax.all_to_all(grid_feats, ('node', 'local'), split_axis=0, concat_axis=0...]
    pallas_call x0 -> x1, Pallas kernels: none -> 173 us  [fused_local(): pl.pallas_call(fused_kernel, out_shape=jax.ShapeDtypeStruct((local_count...]
    dot_general x4 -> x0, matrix products: 36.2 us -> none  [the longest x1 14.9 us: local(): jnp.dot(hidden, hidden_basis[0], preferred_element_type=jnp.float32)]
    unnamed x2 -> x0, waiting for transfers between devices: 28.4 us -> none
    gather x4 -> x0, local copies, waits for them, and re-layouts: 23.4 us -> none  [the longest x1 6.96 us: local(): sent_examples = example_id[token_of].astype(jnp.bfloat16)]
    all_to_all x3 -> x0, starting transfers between devices: 17.1 us -> none  [the longest x1 7.3 us: local(): lax.all_to_all(grid_examples, ('node', 'local'), split_axis=0, concat_axi...]
    convert_element_type x3 -> x0, local copies, waits for them, and re-layouts: 13.1 us -> none  [the longest x1 12.9 us: local(): out_grad[token_of].astype(jnp.float32)]
    convert_element_type x6 -> x0, other arithmetic: 9.24 us -> none  [the longest x1 9.16 us: local(): (weight_of[:, None] * out_grad[token_of].astype(jnp.float32)).astype(jnp....]
  transfers between devices with their start and end apart: 5 -> 0, of which waited for: 4 -> 0; matrix products, arithmetic and copies ran while one was open for 11% -> 0% of each run, Pallas kernels for 0% -> 0%
where the time goes in v1:
time: 186 us; the launch traced here: 185 us
  Pallas kernels  173 us (93%)
  local copies, waits for them, and re-layouts  10.4 us (6%)
  other arithmetic  2.39 us (1%)
    pallas_call x1, Pallas kernels, fused_local(): pl.pallas_call(fused_kernel, out_shape=jax.ShapeDtypeStruct((local_count...  173 us
    unnamed x4, local copies, waits for them, and re-layouts  7.43 us

profile of v1, /device:TPU:0, one launch (start us, length us, event | category | flops | bytes accessed | tf_op | source)
XLA Modules:
  0.0 185.5 jit_solution(6098581751906983115)
XLA Ops:
  0.0 0.0 copy-start
  0.0 0.9 convert_reduce_fusion
  0.9 0.1 pad.2.clone
  1.0 0.1 slice_convert_fusion.1
  1.1 0.1 reshape.11
  1.2 0.1 broadcast_in_dim.37
  1.2 0.1 broadcast_in_dim.38
  1.3 0.1 reshape.12
  1.4 0.1 broadcast_in_dim.40
  1.5 0.1 broadcast_in_dim.41
  1.6 0.7 maximum_maximum_fusion.aux_ref
  2.3 0.7 select_reduce_fusion
  3.0 0.7 copy.22.coef_ref
  3.7 4.6 %copy.20 = bf16[1,2048,704]{2,1,0:T(8,128)(2,1)} copy(bf16[1,2048,704]{1,2,0:T(8,128)(2,1)} %param.14) | data formatting | bytes 5767168 | tf_op args[5]
  8.3 0.0 copy-done
  8.3 2.8 %copy.21 = bf16[1,2048,704]{2,1,0:T(8,128)(2,1)} copy(bf16[1,2048,704]{1,2,0:T(8,128)(2,1)S(1)} %copy-done) | data formatting | bytes 5767168 | tf_op args[6]
  11.1 172.7 %shard_map.91 = f32[2,64,128]{2,1,0:T(8,128)} custom-call(bf16[128,2048]{1,0:T(8,128)(2,1)} %tok_ref.1, bf16[128,2048]{1,0:T(8,128)(2,1)} %grad_ref.1, f32[128,16]{1,0:T(8,128)} %copy.22.coef_ref, bf16[16,128]{1,0:T(8,128)(2,1)} %maximum_maximum_fusion.aux_ref, bf16[2048,704]{1,0:T(8,128)(2,1)} %bitcast.11, bf16[2048,704]{1,0:T(8,128)(2,1)} %bitcast.12, ...), custom_call_target="tpu_custom_call" | custom-call | flops 23622320128 | bytes 8388608 | tf_op jit(solution)/shard_map/pallas_call | solution.py:445
  183.8 1.0 reshape.10
  184.8 0.7 copy.25
  (1 shorter events, 0.0 us)
Async XLA Ops:
  0.0 8.3 %copy-start = (bf16[1,2048,704]{1,2,0:T(8,128)(2,1)S(1)}, bf16[1,2048,704]{1,2,0:T(8,128)(2,1)}, u32[]{:S(2)}) copy-start(bf16[1,2048,704]{1,2,0:T(8,128)(2,1)} %param.15) | copy-start | bytes 8650756

commit v2 on v1

--- a/solution.py
+++ b/solution.py
@@ -115,13 +115,15 @@
 def fused_kernel(
     tok_ref,
     grad_ref,
-    coef_ref,
+    route_ref,
+    weight_ref,
     aux_ref,
     gate_ref,
     up_ref,
     hid_ref,
     basis_ref,
     out_ref,
+    wbuf,
     tbuf,
     qbuf,
     rmsg,
@@ -180,28 +182,29 @@
         pl.semaphore_signal(barrier, inc=1, device_id=where, device_id_type=MESH)
     pl.semaphore_wait(barrier, chips + 1)
 
+    least = jnp.minimum(zi, depth - 1 - zi)
+    lean = jnp.where(zi > depth - 1 - zi, -1, 1)
+
     def place(idx):
-        k, pos = idx // 4, idx % 4
+        n, pos = idx // 4, idx % 4
         one, two = pos % 2, pos // 2
-        away = (k + 1) // 2
-        dz = away * (1 - 2 * (k % 2))
-        oz = zi + dz
-        valid = (oz >= 0) & (oz < depth)
-        oz = jnp.clip(oz, 0, depth - 1)
+        swing = ((n + 1) // 2) * (1 - 2 * (n % 2))
+        dz = jnp.where(n <= 2 * least, swing, lean * (n - least))
+        oz = jnp.clip(zi + dz, 0, depth - 1)
         flip_x = one * first_x + two * first_y
         flip_y = one * first_y + two * first_x
         origin = (oz * 2 + (yi + flip_y) % 2) * 2 + (xi + flip_x) % 2
-        return origin, valid, one, two, dz
+        return origin, one, two, dz
 
     def links(idx, view, send, recv, twin_recv):
-        origin, valid, one, two, dz = place(idx)
-        straight = valid & (one == 0) & (two == 0)
+        origin, one, two, dz = place(idx)
+        straight = (one == 0) & (two == 0)
         plan = (
             (straight & (dz <= 0) & (zi < depth - 1), up, recv),
             (straight & (dz >= 0) & (zi > 0), down, recv),
-            (valid & (two == 0), far, recv),
+            (two == 0, far, recv),
             (straight, near, recv),
-            (valid, twin, twin_recv),
+            (None, twin, twin_recv),
         )
         for j, (wanted, where, sem) in enumerate(plan):
             copy = pltpu.make_async_remote_copy(
@@ -225,18 +228,18 @@
         )
 
     def forward(idx, view, send, recv, twin_recv):
-        origin, valid, *_ = place(idx)
-
-        @pl.when(valid & (idx > 0))
+        origin = place(idx)[0]
+
+        @pl.when(idx > 0)
         def _():
             arrival(view, origin, core, send, recv).wait_recv()
 
         for wanted, copy in links(idx, view, send, recv, twin_recv):
-            pl.when(wanted)(copy.start)
+            copy.start() if wanted is None else pl.when(wanted)(copy.start)
 
     def finish(idx, view, send, recv, twin_recv):
         for wanted, copy in links(idx, view, send, recv, twin_recv):
-            pl.when(wanted)(copy.wait_send)
+            copy.wait_send() if wanted is None else pl.when(wanted)(copy.wait_send)
 
     def t_view(origin, c):
         return tbuf.at[origin, c]
@@ -246,27 +249,17 @@
 
     t_all = (t_view, t_send, t_recv, ts_recv)
     q_all = (q_view, q_send, q_recv, qs_recv)
-    positions = 4 * (2 * depth - 1)
 
     own_q = pltpu.make_async_copy(basis_ref, qbuf.at[core, me], own_sem.at[0])
     own_t = pltpu.make_async_copy(tok_ref, tbuf.at[me, core], own_sem.at[1])
+    own_g = pltpu.make_async_copy(gate_ref, wbuf.at[0], own_sem.at[3])
+    own_u = pltpu.make_async_copy(up_ref, wbuf.at[1], own_sem.at[4])
     own_q.start()
     own_t.start()
-    own_q.wait()
-
-    @pl.loop(0, positions)
-    def _(idx):
-        forward(idx, *q_all)
-
-    own_t.wait()
-    forward(0, *t_all)
-
-    @pl.loop(0, chips)
-    def _(chip):
-        arrival(q_view, chip, 1 - core, q_send, qs_recv).wait_recv()
-
-    @pl.loop(0, chips)
-    def _(chip):
+    own_g.start()
+    own_u.start()
+
+    def project(chip):
         total = None
         for h in (0, 1):
             block = qbuf[h, chip]
@@ -278,8 +271,8 @@
                 preferred_element_type=jnp.float32,
             )
             total = term if total is None else total + term
-        lanes = lax.broadcasted_iota(jnp.int32, coef_ref.shape, 1)
-        column = jnp.sum(jnp.where(lanes == chip, coef_ref[...], 0.0), axis=1, keepdims=True)
+        named = jnp.where(route_ref[...] == chip, weight_ref[...], 0.0)
+        column = jnp.sum(named, axis=1, keepdims=True)
         rmsg[chip, :rows] = (total * column).astype(jnp.bfloat16)
         rmsg[chip, rows:] = aux_ref[...]
 
@@ -294,57 +287,21 @@
         )
 
     own_r = pltpu.make_async_copy(rmsg.at[me], rbuf.at[core, me], own_sem.at[2])
-    own_r.start()
-
-    @pl.loop(1, chips)
-    def _(step):
-        r_copy((me + step) % chips).start()
 
     def compute(origin):
         feats = tbuf[origin].reshape(2 * rows, tok_ref.shape[1])
-        gate = jnp.dot(feats, gate_ref[...], preferred_element_type=jnp.float32)
-        upper = jnp.dot(feats, up_ref[...], preferred_element_type=jnp.float32)
+        gate, upper = (
+            lax.dot_general(
+                wbuf[w], feats, (((1,), (1,)), ((), ())), preferred_element_type=jnp.float32
+            )
+            for w in (0, 1)
+        )
         hidden = (gate / (1.0 + jnp.exp(-gate)) * upper).astype(jnp.bfloat16)
-        left = lax.dot_general(
-            hid_ref[...],
-            hidden,
-            (((1,), (1,)), ((), ())),
-            preferred_element_type=jnp.float32,
-        )
+        left = jnp.dot(hid_ref[...], hidden, preferred_element_type=jnp.float32)
         high = left.astype(jnp.bfloat16)
         low = (left - high.astype(jnp.float32)).astype(jnp.bfloat16)
         lbuf[origin, :rank] = high
         lbuf[origin, rank:] = low
-
-    lag = 2
-
-    @pl.loop(0, positions + lag)
-    def _(idx):
-        @pl.when((idx > 0) & (idx < positions))
-        def _():
-            forward(idx, *t_all)
-
-        earlier = jnp.maximum(idx - lag, 0)
-        origin, valid, *_ = place(earlier)
-
-        @pl.when(valid & (idx >= lag))
-        def _():
-            arrival(t_view, origin, 1 - core, t_send, ts_recv).wait_recv()
-            compute(origin)
-
-    own_r.wait()
-
-    @pl.loop(1, chips)
-    def _(step):
-        chip = (me + step) % chips
-        pltpu.make_async_remote_copy(
-            src_ref=rmsg.at[chip],
-            dst_ref=rbuf.at[core, chip],
-            send_sem=r_send.at[chip],
-            recv_sem=r_recv.at[chip],
-            device_id=twin,
-            device_id_type=MESH,
-        ).wait_recv()
 
     share = pltpu.make_async_remote_copy(
         src_ref=rbuf.at[core],
@@ -354,9 +311,58 @@
         device_id=twin,
         device_id_type=MESH,
     )
-    share.start()
+
+    def q_step(idx):
+        pl.when(idx < chips)(lambda: forward(idx, *q_all))
+
+        @pl.when((idx >= lag) & (idx < chips + lag))
+        def _():
+            chip = place(idx - lag)[0]
+            arrival(q_view, chip, 1 - core, q_send, qs_recv).wait_recv()
+            project(chip)
+            pl.when(chip == me)(own_r.start)
+            pl.when(chip != me)(lambda: r_copy(chip).start())
+
+    lag = 2
+    own_q.wait()
+    forward(0, *q_all)
+    own_t.wait()
+    forward(0, *t_all)
+    forward(1, *q_all)
+    own_g.wait()
+    own_u.wait()
+
+    @pl.loop(1, chips + lag)
+    def _(idx):
+        q_step(2 * idx)
+        q_step(2 * idx + 1)
+        pl.when(idx < chips)(lambda: forward(idx, *t_all))
+
+        @pl.when(idx >= lag)
+        def _():
+            origin = place(idx - lag)[0]
+            arrival(t_view, origin, 1 - core, t_send, ts_recv).wait_recv()
+            compute(origin)
+
+        @pl.when(idx == chips - 2)
+        def _():
+            own_r.wait()
+
+            @pl.loop(1, chips)
+            def _(step):
+                chip = (me + step) % chips
+                pltpu.make_async_remote_copy(
+                    src_ref=rmsg.at[chip],
+                    dst_ref=rbuf.at[core, chip],
+                    send_sem=r_send.at[chip],
+                    recv_sem=r_recv.at[chip],
+                    device_id=twin,
+                    device_id_type=MESH,
+                ).wait_recv()
+
+            share.start()
+
     share.wait_recv()
-
     acc[...] = jnp.zeros_like(acc)
 
     @pl.loop(0, chips)
@@ -396,7 +402,9 @@
     for step in range(1, pairs):
         f_copy(step, True).wait_recv()
     for e in range(pairs // 2):
-        out_ref[e] = fbuf[2 * e] + fbuf[2 * e + 1]
+        pair = fbuf[2 * e] + fbuf[2 * e + 1]
+        out_ref[e, 0] = pair[:, :rank]
+        out_ref[e, 1] = pair[:, rank:]
 
     for step in range(1, pairs):
         f_copy(step, False).wait_send()
@@ -406,7 +414,7 @@
     def _(step):
         r_copy((me + step) % chips).wait_send()
 
-    @pl.loop(0, positions)
+    @pl.loop(0, chips)
     def _(idx):
         finish(idx, *q_all)
         finish(idx, *t_all)
@@ -429,8 +437,6 @@
     rows, width = tokens.shape
     half_width = hidden_basis.shape[1]
     rank = hidden_basis.shape[2]
-    chosen = routes[:, :, None] == jnp.arange(chips, dtype=jnp.int32)
-    coef = jnp.sum(jnp.where(chosen, route_weight[:, :, None], 0.0), axis=1)
     before = jnp.sum(
         example_id[None, :] < jnp.arange(examples + 1, dtype=jnp.int32)[:, None], axis=1
     )
@@ -442,12 +448,13 @@
     dma = pltpu.SemaphoreType.DMA
     bf16, f32 = jnp.bfloat16, jnp.float32
     flops = 2 * 2 * rows * chips * width * 2 * half_width
-    logged = pl.pallas_call(
+    return pl.pallas_call(
         fused_kernel,
-        out_shape=jax.ShapeDtypeStruct((local_count // 2, rank, 2 * rank), f32),
-        in_specs=[vmem] * 8,
+        out_shape=jax.ShapeDtypeStruct((local_count // 2, 2, rank, rank), f32),
+        in_specs=[vmem] * 5 + [pl.BlockSpec(memory_space=pl.ANY)] * 2 + [vmem] * 2,
         out_specs=vmem,
         scratch_shapes=[
+            pltpu.VMEM((2, half_width, width), bf16),
             pltpu.VMEM((chips, 2, rows, width), bf16),
             pltpu.VMEM((2, chips, rank, width // 2), bf16),
             pltpu.VMEM((chips, rows + 16, 2 * rank), bf16),
@@ -456,7 +463,7 @@
             pltpu.VMEM((2 * rank, examples * rank), f32),
             pltpu.VMEM((local_count, rank, 2 * rank), f32),
             pltpu.VMEM((local_count, rank, 2 * rank), f32),
-            dma((3,)),
+            dma((5,)),
             dma((chips, 5)),
             dma((chips,)),
             dma((chips,)),
@@ -476,15 +483,14 @@
     )(
         tokens,
         out_grad,
-        coef,
+        routes,
+        route_weight,
         aux,
-        gate_weight[0],
-        up_weight[0],
+        gate_weight[0].T,
+        up_weight[0].T,
         hidden_basis[0].T,
         model_basis[0].T,
     )
-    logged = logged.reshape(local_count // 2, rank, 2, rank)
-    return logged.transpose(0, 2, 1, 3)
 
 
 def solution(mesh):

time: 186 us -> 160 us (0.86)
  Pallas kernels: 173 us -> 153 us
  local copies, waits for them, and re-layouts: 10.4 us -> 4.97 us
    pallas_call x1, Pallas kernels: 173 us -> 153 us  [fused_local(): pl.pallas_call(fused_kernel, out_shape=jax.ShapeDtypeStruct((local_count...]
    unnamed x4 -> x3, local copies, waits for them, and re-layouts: 7.43 us -> 4.4 us
where the time goes in v2:
time: 160 us; the launch traced here: 159 us
  Pallas kernels  153 us (96%)
  local copies, waits for them, and re-layouts  4.97 us (3%)
    pallas_call x1, Pallas kernels, fused_local(): pl.pallas_call(fused_kernel, out_shape=jax.ShapeDtypeStruct((local_count...  153 us
    unnamed x3, local copies, waits for them, and re-layouts  4.4 us

profile of v2, /device:TPU:0, one launch (start us, length us, event | category | flops | bytes accessed | tf_op | source)
XLA Modules:
  0.0 159.4 jit_solution(3623468446111401933)
XLA Ops:
  0.0 0.8 convert_reduce_fusion
  0.8 0.1 pad.2.clone
  0.9 0.1 slice_convert_fusion.1
  0.9 0.1 reshape.5
  1.0 0.1 broadcast_in_dim.20
  1.1 0.1 broadcast_in_dim.21
  1.2 0.1 reshape.6
  1.3 0.1 broadcast_in_dim.23
  1.3 0.1 broadcast_in_dim.24
  1.4 0.7 maximum_maximum_fusion.aux_ref
  2.1 1.4 copy.14.route_ref
  3.5 1.4 copy.15.weight_ref
  4.9 152.9 %shard_map.91 = f32[2,2,64,64]{3,2,1,0:T(8,128)} custom-call(bf16[128,2048]{1,0:T(8,128)(2,1)} %tok_ref.1, bf16[128,2048]{1,0:T(8,128)(2,1)} %grad_ref.1, s32[128,6]{1,0:T(8,128)} %copy.14.route_ref, f32[128,6]{1,0:T(8,128)} %copy.15.weight_ref, bf16[16,128]{1,0:T(8,128)(2,1)} %maximum_maximum_fusion.aux_ref, bf16[704,2048]{1,0:T(8,128)(2,1)} %bitcast.12, ...), custom_call_target="tpu_custom_call" | custom-call | flops 23622320128 | bytes 8388608 | tf_op jit(solution)/shard_map/pallas_call | solution.py:451
  157.8 1.6 copy.17
  (1 shorter events, 0.0 us)

commit v3 on v2

--- a/solution.py
+++ b/solution.py
@@ -199,11 +199,14 @@
     def links(idx, view, send, recv, twin_recv):
         origin, one, two, dz = place(idx)
         straight = (one == 0) & (two == 0)
+        beside = (one == 1) & (two == 0)
+        climb = (straight & (dz <= 0)) | (beside & (dz < 0))
+        fall = (straight & (dz >= 0)) | (beside & (dz > 0))
         plan = (
-            (straight & (dz <= 0) & (zi < depth - 1), up, recv),
-            (straight & (dz >= 0) & (zi > 0), down, recv),
+            (climb & (zi < depth - 1), up, recv),
+            (fall & (zi > 0), down, recv),
             (two == 0, far, recv),
-            (straight, near, recv),
+            (straight & (dz >= -1) & (dz <= 1), near, recv),
             (None, twin, twin_recv),
         )
         for j, (wanted, where, sem) in enumerate(plan):

time: 160 us -> 158 us (0.988)
  Pallas kernels: 153 us -> 151 us
    pallas_call x1, Pallas kernels: 153 us -> 151 us  [fused_local(): pl.pallas_call(fused_kernel, out_shape=jax.ShapeDtypeStruct((local_count...]
where the time goes in v3:
time: 158 us
  Pallas kernels  151 us (96%)
  local copies, waits for them, and re-layouts  4.97 us (3%)
    pallas_call x1, Pallas kernels, fused_local(): pl.pallas_call(fused_kernel, out_shape=jax.ShapeDtypeStruct((local_count...  151 us
    unnamed x3, local copies, waits for them, and re-layouts  4.4 us

profile of v3, /device:TPU:0, one launch (start us, length us, event | category | flops | bytes accessed | tf_op | source)
XLA Modules:
  0.0 157.8 jit_solution(3970598161945359455)
XLA Ops:
  0.0 0.8 convert_reduce_fusion
  0.8 0.1 pad.2.clone
  0.9 0.1 slice_convert_fusion.1
  0.9 0.1 reshape.5
  1.0 0.1 broadcast_in_dim.20
  1.1 0.1 broadcast_in_dim.21
  1.2 0.1 reshape.6
  1.3 0.1 broadcast_in_dim.23
  1.3 0.1 broadcast_in_dim.24
  1.4 0.7 maximum_maximum_fusion.aux_ref
  2.1 1.4 copy.14.route_ref
  3.5 1.4 copy.15.weight_ref
  4.9 151.3 %shard_map.91 = f32[2,2,64,64]{3,2,1,0:T(8,128)} custom-call(bf16[128,2048]{1,0:T(8,128)(2,1)} %tok_ref.1, bf16[128,2048]{1,0:T(8,128)(2,1)} %grad_ref.1, s32[128,6]{1,0:T(8,128)} %copy.14.route_ref, f32[128,6]{1,0:T(8,128)} %copy.15.weight_ref, bf16[16,128]{1,0:T(8,128)(2,1)} %maximum_maximum_fusion.aux_ref, bf16[704,2048]{1,0:T(8,128)(2,1)} %bitcast.12, ...), custom_call_target="tpu_custom_call" | custom-call | flops 23622320128 | bytes 8388608 | tf_op jit(solution)/shard_map/pallas_call | solution.py:454
  156.2 1.6 copy.17
  (1 shorter events, 0.0 us)
